TPU v7x, 128 devices: a whole 4x4x4 slice. The times are simulated.
128 devices in a mesh: row: 8 (over z, y_hi), col: 16 (over x, y_lo, core).
Axes of the slice: x: 4, y: 4 (y_hi: 2, y_lo: 2; y = y_hi * 2 + y_lo), z: 4, core: 2. Of those that a mesh axis runs over, the one named last changes fastest.
Arguments:
- left: bfloat16 [16, 32, 2048], P('col', None, 'row'), may hold values from -6 to 6
- right: bfloat16 [16, 32, 2048], P('row', None, 'col'), may hold values from -6 to 6
- pair_grad: bfloat16 [2048, 2048, 128], P('row', 'col'), may hold values from -3 to 3
- w_out: bfloat16 [1024, 128], replicated, may hold values from -0.1875 to 0.1875
Outputs:
- d_left: float32 [16, 32, 2048], P('col', None, 'row')
- d_right: float32 [16, 32, 2048], P('row', None, 'col')
- d_wout: float32 [1024, 128], replicated
All inputs are finite; a program needn't handle non-finite values.
Results may differ from a plain program's by a relative error of at most 0.0095.
Values may be sent and summed in bfloat16 or wider, within the bound.
A program may use at most 192 MiB of HBM per device.

v0:
```python
import jax
import jax.numpy as jnp
from jax import lax
from jax.sharding import PartitionSpec as P


def on_device(left, right, pair_grad, w_out):
    left_full = lax.all_gather(left, "col", axis=0, tiled=True)
    right_full = lax.all_gather(right, "row", axis=0, tiled=True)
    seqs, chans, rows = left_full.shape
    cols = right_full.shape[2]
    pairch = pair_grad.shape[2]
    total_rows = rows * lax.axis_size("row")
    total_cols = cols * lax.axis_size("col")
    cube = w_out.reshape(chans, chans, pairch)
    ublock = jnp.einsum("sej,ceh->jhsc", right_full, cube, preferred_element_type=jnp.float32)
    ublock = ublock.astype(jnp.bfloat16).reshape(cols * pairch, seqs * chans)
    part_left = jnp.dot(
        pair_grad.reshape(rows, cols * pairch), ublock, preferred_element_type=jnp.float32
    )
    part_left = part_left.reshape(rows, seqs, chans).transpose(1, 2, 0)
    wblock = jnp.einsum(
        "sci,ceh->ihse", left_full, cube, preferred_element_type=jnp.float32
    ).astype(jnp.bfloat16)
    part_right = lax.dot_general(
        pair_grad, wblock, (((0, 2), (0, 1)), ((), ())), preferred_element_type=jnp.float32
    )
    part_right = part_right.transpose(1, 2, 0)
    vblock = lax.dot_general(
        pair_grad, right_full, (((1,), (2,)), ((), ())), preferred_element_type=jnp.float32
    )
    vblock = vblock.astype(jnp.bfloat16)
    part_weight = jnp.einsum("sci,ihse->ceh", left_full, vblock, preferred_element_type=jnp.float32)
    part_weight = part_weight.reshape(chans * chans, pairch)
    summed_right = lax.psum_scatter(part_right, "row", scatter_dimension=0, tiled=True)
    summed_left = lax.psum_scatter(part_left, "col", scatter_dimension=0, tiled=True)
    summed_weight = lax.psum(part_weight, ("row", "col"))
    grad_left = summed_left * (1.0 / seqs)
    grad_right = summed_right * (1.0 / seqs)
    grad_weight = summed_weight * (1.0 / (float(total_rows) * float(total_cols)) ** 0.5)
    return (grad_left, grad_right, grad_weight)


def solution(mesh):
    return jax.shard_map(
        on_device,
        mesh=mesh,
        in_specs=(P("col", None, "row"), P("row", None, "col"), P("row", "col", None), P()),
        out_specs=(P("col", None, "row"), P("row", None, "col"), P()),
        check_vma=False,
    )
```

profile of v0, /device:TPU:0, one launch (start us, length us, event | category | flops | bytes accessed | tf_op | source)
XLA Modules:
  0.0 333.2 jit_solution(12305938278311064865)
XLA Ops:
  8.0 0.0 all-reduce.2.cloned.1.call-start
  8.0 36.0 %all_gather.6 = bf16[16,32,128]{2,1,0:T(8,128)(2,1)S(1)} all-gather(bf16[2,32,128]{2,1,0:T(8,128)(2,1)} %param.5), channel_id=1, replica_groups=mesh['row'=8,'col'=16] {'row'}, dimensions={0}, use_global_device_ids=true | all-gather | bytes 147456 | tf_op jit(solution)/shard_map/all_gather | solution.py:9
  44.0 20.7 %all_gather.7 = bf16[16,32,256]{2,1,0:T(8,128)(2,1)S(1)} all-gather(bf16[1,32,256]{2,1,0:T(8,128)(2,1)} %param.4), channel_id=1, replica_groups=mesh['row'=8,'col'=16] {'col'}, dimensions={0}, use_global_device_ids=true | all-gather | bytes 278528 | tf_op jit(solution)/shard_map/all_gather | solution.py:8
  64.7 17.4 %convolution_convert_fusion = bf16[256,128,16,32]{1,3,2,0:T(8,128)(2,1)} fusion(bf16[256,128,128]{2,1,0:T(8,128)(2,1)} %param.6, bf16[16,32,128]{2,1,0:T(8,128)(2,1)S(1)} %all_gather.6), kind=kOutput, calls=%fused_computation.3 | convolution fusion | flops 4311744512 | bytes 42074112 | tf_op jit(solution)/shard_map/dot_general | solution.py:29
  82.1 0.0 copy-start
  82.1 33.0 %fusion.10 = f32[32,32,128]{2,0,1:T(8,128)S(1)} fusion(bf16[256,128,16,32]{1,3,2,0:T(8,128)(2,1)} %convolution_convert_fusion, bf16[16,32,256]{2,1,0:T(8,128)(2,1)S(1)} %all_gather.7), kind=kOutput, calls=%fused_computation.13 | convolution fusion | flops 1073741824 | bytes 34340864 | tf_op jit(solution)/shard_map/sci,ihse->ceh/dot_general | solution.py:33
  115.1 1.1 copy.13
  116.2 0.0 all-reduce.2.cloned.1.call-update
  116.3 0.0 reduce-scatter.5.cloned.1.call-start
  116.3 0.0 copy-done
  116.3 13.8 %convert_bitcast_fusion = bf16[256,128,16,32]{0,1,2,3:T(8,128)(2,1)} fusion(bf16[16,32,256]{2,1,0:T(8,128)(2,1)S(1)} %all_gather.7, bf16[32,32,128,1]{2,1,0,3:T(8,128)(2,1)S(1)} %bitcast.59), kind=kOutput, calls=%fused_computation.2 | convolution fusion | flops 1090519040 | bytes 34078720 | tf_op jit(solution)/shard_map/sci,ceh->ihse/dot_general | solution.py:22
  130.1 45.5 %copy.11 = bf16[256,128,16,32]{1,3,0,2:T(8,128)(2,1)} copy(bf16[256,128,16,32]{0,1,2,3:T(8,128)(2,1)} %convert_bitcast_fusion) | data formatting | bytes 67108864 | tf_op jit(solution)/shard_map/convert_element_type | solution.py:24
  175.6 18.2 %fusion.13 = f32[16,32,128]{2,1,0:T(8,128)} fusion(bf16[256,128,16,32]{1,3,0,2:T(8,128)(2,1)} %copy.11, bf16[256,128,128]{2,1,0:T(8,128)(2,1)} %param.6), kind=kOutput, calls=%fused_computation.14 | convolution fusion | flops 4294967296 | bytes 42205184 | tf_op jit(solution)/shard_map/dot_general | solution.py:25
  193.7 0.0 reduce-scatter.5.cloned.1.call-update
  193.8 0.0 reduce-scatter.3.cloned.1.call-start
  193.8 8.1 %convert_bitcast_fusion.1 = bf16[128,128,16,32]{0,1,2,3:T(8,128)(2,1)} fusion(bf16[32,32,128,1]{2,1,3,0:T(8,128)(2,1)S(1)} %bitcast.60, bf16[16,32,128]{2,1,0:T(8,128)(2,1)S(1)} %all_gather.6), kind=kOutput, calls=%fused_computation.7 | convolution fusion | flops 545259520 | bytes 17170432 | tf_op jit(solution)/shard_map/sej,ceh->jhsc/dot_general | solution.py:16
  201.9 21.2 %copy.9 = bf16[128,128,16,32]{1,0,3,2:T(8,128)(2,1)} copy(bf16[128,128,16,32]{0,1,2,3:T(8,128)(2,1)} %convert_bitcast_fusion.1) | data formatting | bytes 33554432 | tf_op jit(solution)/shard_map/convert_element_type | solution.py:17
  223.2 26.6 %fusion.2 = f32[512,256]{1,0:T(8,128)} fusion(bf16[64,8,128,128]{3,2,1,0:T(8,128)(2,1)} %bitcast.56, bf16[32,8,128,128]{3,2,1,0:T(8,128)(2,1)} %bitcast.57), kind=kOutput, calls=%fused_computation.4 | convolution fusion | flops 4294967296 | bytes 25690112 | tf_op jit(solution)/shard_map/dot_general | solution.py:18
  249.7 0.0 reduce-scatter.3.cloned.1.call-update
  249.8 9.6 %all-reduce.2.cloned.1.call-done = f32[1024,128]{1,0:T(8,128)} async-done(((f32[1024,128]{1,0:T(8,128)}), f32[1024,128]{1,0:T(8,128)}) %all-reduce.2.cloned.1.call-update) | async-done | bytes 524304 | tf_op jit(solution)/shard_map/psum | solution.py:37
  259.4 1.9 broadcast_multiply_fusion
  261.2 1.2 reduce-scatter.5.cloned.1.call-done
  262.5 1.4 broadcast_multiply_fusion.1
  263.9 60.3 %reduce-scatter.3.cloned.1.call-done = f32[1,32,256]{2,1,0:T(8,128)} async-done(((f32[16,32,256]{2,1,0:T(8,128)}), f32[1,32,256]{2,1,0:T(8,128)}) %reduce-scatter.3.cloned.1.call-update) | async-done | bytes 32784 | tf_op jit(solution)/shard_map/reduce_scatter | solution.py:36
  324.2 1.4 broadcast_multiply_fusion.2
Async XLA Ops:
  8.0 251.4 %all-reduce.2.cloned.1.call-start = ((), (), s32[]{:S(2)}) async-start(), calls=%async_computation.4 | async-start | bytes 1048576 | tf_op jit(solution)/shard_map/psum | solution.py:37
  82.1 34.2 %copy-start = (bf16[1024,128]{1,0:T(8,128)(2,1)S(1)}, bf16[1024,128]{1,0:T(8,128)(2,1)}, u32[]{:S(2)}) copy-start(bf16[1024,128]{1,0:T(8,128)(2,1)} %param.7) | copy-start | bytes 786436
  116.3 146.2 %reduce-scatter.5.cloned.1.call-start = ((), (), s32[]{:S(2)}) async-start(), calls=%async_computation.3 | async-start | bytes 294912 | tf_op jit(solution)/shard_map/reduce_scatter | solution.py:35
  193.8 130.4 %reduce-scatter.3.cloned.1.call-start = ((), (), s32[]{:S(2)}) async-start(), calls=%async_computation.2 | async-start | bytes 557056 | tf_op jit(solution)/shard_map/reduce_scatter | solution.py:36
Sparse Core Ops, SparseCore 0:
  116.4 142.9 all-reduce.1
Sparse Core Ops, SparseCore 1:
  193.8 68.6 reduce-scatter.4
  264.7 59.4 reduce-scatter.2
where the time goes:
time: 338 us; the launch traced here: 333 us
  matrix products  117 us (35%)
  waiting for transfers between devices  71.2 us (21%)
  local copies, waits for them, and re-layouts  67.8 us (20%)
  blocking collectives  56.6 us (17%)
  between operations  15.7 us (5%)
  other arithmetic  4.62 us (1%)
    reduce_scatter x1, waiting for transfers between devices, on_device(): lax.psum_scatter(part_left, 'col', scatter_dimension=0, tiled=True)  60.3 us
    convert_element_type x1, local copies, waits for them, and re-layouts, on_device(): wblock = jnp.einsum('sci,ceh->ihse', left_full, cube, preferred_element_t...  45.5 us
    all_gather x1, blocking collectives, on_device(): right_full = lax.all_gather(right, 'row', axis=0, tiled=True)  36 us
    dot_general x1, matrix products, on_device(): jnp.einsum('sci,ihse->ceh', left_full, vblock, preferred_element_type=jnp...  33 us
    dot_general x1, matrix products, on_device(): jnp.dot(pair_grad.reshape(rows, cols * pairch), ublock, preferred_element...  26.6 us
    convert_element_type x1, local copies, waits for them, and re-layouts, on_device(): ublock = ublock.astype(jnp.bfloat16).reshape(cols * pairch, seqs * chans)  21.2 us
    all_gather x1, blocking collectives, on_device(): left_full = lax.all_gather(left, 'col', axis=0, tiled=True)  20.7 us
    dot_general x1, matrix products, on_device(): lax.dot_general(pair_grad, wblock, (((0, 2), (0, 1)), ((), ())), preferre...  18.2 us
  transfers between devices with their start and end apart: 3, of which 3 were waited for; matrix products, arithmetic and copies ran while one was open for 41% of the time, Pallas kernels for 0%

commit v1 on v0

v1 whole, which is shorter than its diff:
```python
import functools

import jax
import jax.numpy as jnp
from jax import lax
from jax.experimental import pallas as pl
from jax.experimental.pallas import tpu as pltpu
from jax.sharding import PartitionSpec as P

BF, F32 = jnp.bfloat16, jnp.float32
MESH = pl.DeviceIdType.MESH
S, C, H = 16, 32, 128
IL, JL = 256, 128
NR, NC = 8, 16
JB = 16
NB = JL // JB
BLK = JB * S


def dot_nn(a, b):
    return jnp.dot(a, b, preferred_element_type=F32)


def dot_nt(a, b):
    return lax.dot_general(a, b, (((1,), (1,)), ((), ())), preferred_element_type=F32)


def loop(lower, upper, body):
    def step(k, carry):
        body(k)
        return carry

    lax.fori_loop(lower, upper, step, 0)


def kernel(
    scale_weight,
    left_hbm, right_hbm, g_hbm, w_hbm,
    dl_out, dr_out, dw_out,
    w_v, lg, rg, g_in, gt, lf, lb, rf, rb, rt, w1, wt, tb, ub,
    drf, drs, drr, dwa, dws, dwr1, dwp, dws2, dwr2, dwp2, dwg, dla, dls, dlr,
    g_sem, in_sem,
    agl_s, agl_r, agr_s, agr_r, rsr_s, rsr_r, w1_s, w1_r, w2_s, w2_r, w3_s, w3_r, w4_s, w4_r, rsl_s, rsl_r,
):
    me_r = lax.axis_index("row")
    me_c = lax.axis_index("col")

    def row_peer(d):
        return lax.rem(me_r + d, NR)

    def col_peer(d):
        return lax.rem(me_c + d, NC)

    def to_row(src, dst, send, recv, d):
        return pltpu.make_async_remote_copy(
            src_ref=src, dst_ref=dst, send_sem=send.at[d - 1], recv_sem=recv.at[d - 1],
            device_id=(row_peer(d), me_c), device_id_type=MESH,
        )

    def to_col(src, dst, send, recv, d):
        return pltpu.make_async_remote_copy(
            src_ref=src, dst_ref=dst, send_sem=send.at[d - 1], recv_sem=recv.at[d - 1],
            device_id=(me_r, col_peer(d)), device_id_type=MESH,
        )

    barrier = pltpu.get_barrier_semaphore()
    loop(1, NR, lambda d: pl.semaphore_signal(barrier, inc=1, device_id=(row_peer(d), me_c), device_id_type=MESH))
    loop(1, NC, lambda d: pl.semaphore_signal(barrier, inc=1, device_id=(me_r, col_peer(d)), device_id_type=MESH))

    def g_copy(b):
        at = pl.multiple_of(b * JB, JB)
        return pltpu.make_async_copy(g_hbm.at[:, pl.ds(at, JB), :], g_in.at[b], g_sem.at[b])

    local = [
        pltpu.make_async_copy(w_hbm, w_v, in_sem.at[0]),
        pltpu.make_async_copy(left_hbm.at[0], lg.at[me_c], in_sem.at[1]),
        pltpu.make_async_copy(right_hbm, rg.at[pl.ds(2 * me_r, 2)], in_sem.at[2]),
    ]
    for copy in local:
        copy.start()
    loop(0, NB, lambda b: g_copy(b).start())
    pl.semaphore_wait(barrier, NR - 1 + NC - 1)

    def gather_left(d):
        return to_col(left_hbm.at[0], lg.at[me_c], agl_s, agl_r, d)

    def gather_right(d):
        return to_row(right_hbm, rg.at[pl.ds(2 * me_r, 2)], agr_s, agr_r, d)

    loop(1, NC, lambda d: gather_left(d).start())
    loop(1, NR, lambda d: gather_right(d).start())

    local[0].wait()
    for c in range(C):
        w1[:, c * H : (c + 1) * H] = w_v[c * C : (c + 1) * C, :]
        block = w_v[c * C : (c + 1) * C, :].astype(F32)
        wt[c * H : (c + 1) * H, :] = jnp.concatenate([block, jnp.zeros((128 - C, H), F32)], 0).T.astype(BF)
    dwa[...] = jnp.zeros_like(dwa)
    dla[...] = jnp.zeros_like(dla)

    def turn(b):
        g_copy(b).wait()
        for q in range(IL // 16):
            gt[b, :, q * 16 : (q + 1) * 16, :] = jnp.swapaxes(g_in[b, q * 16 : (q + 1) * 16], 0, 1)

    loop(0, NB, turn)

    local[2].wait()
    loop(1, NR, lambda d: gather_right(d).wait())
    for s in range(S):
        block = jnp.concatenate([rg[s].astype(F32), jnp.zeros((128 - C, JL), F32)], 0)
        rf[pl.ds(s, JL, stride=S), :] = block.T
    rb[...] = rf[...].astype(BF)

    def right_turned(b):
        at = pl.multiple_of(b * BLK, BLK)
        rt[:, pl.ds(at, BLK)] = rf[pl.ds(at, BLK), :].T[:C].astype(BF)

    loop(0, NB, right_turned)

    local[1].wait()
    loop(1, NC, lambda d: gather_left(d).wait())
    for s in range(S):
        for k in range(2):
            lf[k, pl.ds(s, C, stride=S), :] = lg[s, :, k * 128 : (k + 1) * 128].astype(F32)
    for k in range(2):
        lb[:, k * 128 : (k + 1) * 128] = lf[k].astype(BF)

    def phase1(b):
        at = pl.multiple_of(b * BLK, BLK)
        for p in range(JB // 2):
            rhs = jnp.concatenate([gt[b, 2 * p], gt[b, 2 * p + 1]], 1)
            t = dot_nn(lb[...], rhs).astype(BF)
            for k in range(2):
                j = 2 * p + k
                for c in range(C):
                    tb[j * S : (j + 1) * S, c * H : (c + 1) * H] = t[c * S : (c + 1) * S, k * H : (k + 1) * H]
        dwa[...] += dot_nn(rt[:, pl.ds(at, BLK)], tb[...])
        drf[pl.ds(at, BLK), :] = dot_nn(tb[...], wt[...])

    loop(0, NB, phase1)

    for c in range(C):
        dws[c * C : (c + 1) * C, :] = dwa[:, c * H : (c + 1) * H].astype(BF)

    def weight_rows(k):
        return pl.ds(pl.multiple_of(k * 64, 64), 64)

    def weight1(d):
        return to_col(dws.at[weight_rows(col_peer(d))], dwr1.at[d - 1], w1_s, w1_r, d)

    loop(1, NC, lambda d: weight1(d).start())
    for s in range(S):
        drs[s] = drf[pl.ds(s, JL, stride=S), :].T[:C].astype(BF)

    def reduce_right(d):
        return to_row(drs.at[pl.ds(2 * row_peer(d), 2)], drr.at[d - 1], rsr_s, rsr_r, d)

    loop(1, NR, lambda d: reduce_right(d).start())

    def weight2(d):
        return to_row(dws2.at[row_peer(d)], dwr2.at[d - 1], w2_s, w2_r, d)

    def weight3(d):
        return to_row(dwp2, dwp.at[me_r], w3_s, w3_r, d)

    def weight4(d):
        return to_col(dwg.at[weight_rows(me_c)], dwg.at[weight_rows(me_c)], w4_s, w4_r, d)

    def stage_a():
        loop(1, NC, lambda d: weight1(d).wait())
        total = dws[weight_rows(me_c), :].astype(F32)
        for k in range(NC - 1):
            total += dwr1[k].astype(F32)
        dws2[...] = total.reshape(NR, 8, H)
        loop(1, NR, lambda d: weight2(d).start())

    def stage_b():
        loop(1, NR, lambda d: weight2(d).wait())
        total = dws2[me_r]
        for k in range(NR - 1):
            total += dwr2[k]
        total = total * scale_weight
        dwp2[...] = total
        dwp[me_r] = total
        loop(1, NR, lambda d: weight3(d).start())

    def stage_c():
        loop(1, NR, lambda d: weight3(d).wait())
        dwg[weight_rows(me_c), :] = dwp[...].reshape(64, H).astype(BF)
        loop(1, NC, lambda d: weight4(d).start())

    def stage_d():
        loop(1, NR, lambda d: reduce_right(d).wait())
        total = drs[pl.ds(2 * me_r, 2)].astype(F32)
        for k in range(NR - 1):
            total += drr[k].astype(F32)
        dr_out[...] = total * (1.0 / S)

    def phase2(b):
        at = pl.multiple_of(b * BLK, BLK)
        for q in range(4):
            u = dot_nn(rb[pl.ds(at, BLK), :C], w1[:, q * 1024 : (q + 1) * 1024]).astype(BF)
            for j in range(JB):
                for c in range(8):
                    row = (q * 8 + c) * S
                    ub[row : row + S, j * H : (j + 1) * H] = u[j * S : (j + 1) * S, c * H : (c + 1) * H]
        rhs = jnp.concatenate([gt[b, j] for j in range(JB)], 1)
        part = dot_nt(ub[...], rhs)
        for k in range(2):
            dla[k] += part[:, k * 128 : (k + 1) * 128]
        pl.when(b == 2)(stage_a)
        pl.when(b == 4)(stage_b)
        pl.when(b == 5)(stage_c)
        pl.when(b == 6)(stage_d)

    loop(0, NB, phase2)

    for s in range(S):
        for k in range(2):
            dls[s, :, k * 128 : (k + 1) * 128] = dla[k, pl.ds(s, C, stride=S), :].astype(BF)

    def reduce_left(d):
        return to_col(dls.at[col_peer(d)], dlr.at[d - 1], rsl_s, rsl_r, d)

    loop(1, NC, lambda d: reduce_left(d).start())
    loop(1, NC, lambda d: weight4(d).wait())
    dw_out[...] = dwg[...].astype(F32)
    loop(1, NC, lambda d: reduce_left(d).wait())
    total = dls[me_c].astype(F32)
    for k in range(NC - 1):
        total += dlr[k].astype(F32)
    dl_out[0] = total * (1.0 / S)


def on_device(left, right, pair_grad, w_out):
    total_rows = pair_grad.shape[0] * lax.axis_size("row")
    total_cols = pair_grad.shape[1] * lax.axis_size("col")
    scale_weight = 1.0 / (float(total_rows) * float(total_cols)) ** 0.5
    sems = [pltpu.SemaphoreType.DMA((n - 1,)) for n in (NC, NR, NR, NC, NR, NR, NC, NC) for _ in range(2)]
    return pl.pallas_call(
        functools.partial(kernel, scale_weight),
        out_shape=(
            jax.ShapeDtypeStruct((1, C, IL), F32),
            jax.ShapeDtypeStruct((2, C, JL), F32),
            jax.ShapeDtypeStruct((C * C, H), F32),
        ),
        in_specs=[pl.BlockSpec(memory_space=pl.ANY)] * 4,
        out_specs=[pl.BlockSpec(memory_space=pltpu.VMEM)] * 3,
        scratch_shapes=[
            pltpu.VMEM((C * C, H), BF),
            pltpu.VMEM((S, C, IL), BF),
            pltpu.VMEM((S, C, JL), BF),
            pltpu.VMEM((NB, IL, JB, H), BF),
            pltpu.VMEM((NB, JB, IL, H), BF),
            pltpu.VMEM((2, C * S, 128), F32),
            pltpu.VMEM((C * S, IL), BF),
            pltpu.VMEM((JL * S, 128), F32),
            pltpu.VMEM((JL * S, 128), BF),
            pltpu.VMEM((C, JL * S), BF),
            pltpu.VMEM((C, C * H), BF),
            pltpu.VMEM((C * H, 128), BF),
            pltpu.VMEM((BLK, C * H), BF),
            pltpu.VMEM((C * S, JB * H), BF),
            pltpu.VMEM((JL * S, 128), F32),
            pltpu.VMEM((S, C, JL), BF),
            pltpu.VMEM((NR - 1, 2, C, JL), BF),
            pltpu.VMEM((C, C * H), F32),
            pltpu.VMEM((C * C, H), BF),
            pltpu.VMEM((NC - 1, 64, H), BF),
            pltpu.VMEM((NR, 8, H), F32),
            pltpu.VMEM((NR, 8, H), F32),
            pltpu.VMEM((NR - 1, 8, H), F32),
            pltpu.VMEM((8, H), F32),
            pltpu.VMEM((C * C, H), BF),
            pltpu.VMEM((2, C * S, 128), F32),
            pltpu.VMEM((S, C, IL), BF),
            pltpu.VMEM((NC - 1, C, IL), BF),
            pltpu.SemaphoreType.DMA((NB,)),
            pltpu.SemaphoreType.DMA((3,)),
            *sems,
        ],
        compiler_params=pltpu.CompilerParams(
            collective_id=0, has_side_effects=True, vmem_limit_bytes=60 * 2**20
        ),
        name="outer_product_mean_grad",
    )(left, right, pair_grad, w_out)


def solution(mesh):
    return jax.shard_map(
        on_device,
        mesh=mesh,
        in_specs=(P("col", None, "row"), P("row", None, "col"), P("row", "col", None), P()),
        out_specs=(P("col", None, "row"), P("row", None, "col"), P()),
        check_vma=False,
    )
```

time: 338 us -> 61.2 us (0.18)
  the two profiles are of different devices: /device:TPU:0 before, /device:TPU:1 now
where the time goes in v1:
time: 61.2 us; the launch traced here: 60.9 us
  Pallas kernels  55.7 us (91%)
  local copies, waits for them, and re-layouts  4.62 us (8%)
  between operations  0.64 us (1%)
    pallas_call x1, Pallas kernels, on_device(): pl.pallas_call(functools.partial(kernel, scale_weight), out_shape=(jax.Sh...  55.7 us
    unnamed x3, local copies, waits for them, and re-layouts  4.62 us

profile of v1, /device:TPU:1, one launch (start us, length us, event | category | flops | bytes accessed | tf_op | source)
XLA Modules:
  0.0 60.9 jit_solution(9436164606164602049)
XLA Ops:
  0.6 55.7 %outer_product_mean_grad.1 = (f32[1,32,256]{2,1,0:T(8,128)}, f32[2,32,128]{2,1,0:T(8,128)}, f32[1024,128]{1,0:T(8,128)}) custom-call(bf16[1,32,256]{2,1,0:T(8,128)(2,1)} %left_hbm.1, bf16[2,32,128]{2,1,0:T(8,128)(2,1)} %right_hbm.1, bf16[256,128,128]{2,1,0:T(8,128)(2,1)} %g_hbm.1, bf16[1024,128]{1,0:T(8,128)(2,1)} %w_hbm.1), custom_call_target="tpu_custom_call" | custom-call | tf_op jit(solution)/shard_map/outer_product_mean_grad/pallas_call | solution.py:241
  56.3 1.4 %copy.10 = f32[1,32,256]{2,1,0:T(8,128)} copy(f32[1,32,256]{2,1,0:T(8,128)} %get-tuple-element.6) | data formatting | bytes 65536
  57.7 1.4 %copy.11 = f32[2,32,128]{2,1,0:T(8,128)} copy(f32[2,32,128]{2,1,0:T(8,128)} %get-tuple-element.7) | data formatting | bytes 65536
  59.1 1.9 %copy.12 = f32[1024,128]{1,0:T(8,128)} copy(f32[1024,128]{1,0:T(8,128)} %get-tuple-element.8) | data formatting | bytes 1048576

commit v2 on v1

--- a/solution.py
+++ b/solution.py
@@ -15,6 +15,8 @@
 JB = 16
 NB = JL // JB
 BLK = JB * S
+NU = 3
+STAGE_A, STAGE_B = 5, 3
 
 
 def dot_nn(a, b):
@@ -38,9 +40,9 @@
     left_hbm, right_hbm, g_hbm, w_hbm,
     dl_out, dr_out, dw_out,
     w_v, lg, rg, g_in, gt, lf, lb, rf, rb, rt, w1, wt, tb, ub,
-    drf, drs, drr, dwa, dws, dwr1, dwp, dws2, dwr2, dwp2, dwg, dla, dls, dlr,
+    drf, drs, drr, dwa, dws, dwr1, dwr2, dwg, dla, dls, dlr,
     g_sem, in_sem,
-    agl_s, agl_r, agr_s, agr_r, rsr_s, rsr_r, w1_s, w1_r, w2_s, w2_r, w3_s, w3_r, w4_s, w4_r, rsl_s, rsl_r,
+    agl_s, agl_r, agr_s, agr_r, rsr_s, rsr_r, w1_s, w1_r, w2_s, w2_r, w3_s, w3_r, rsl_s, rsl_r,
 ):
     me_r = lax.axis_index("row")
     me_c = lax.axis_index("col")
@@ -87,8 +89,8 @@
     def gather_right(d):
         return to_row(right_hbm, rg.at[pl.ds(2 * me_r, 2)], agr_s, agr_r, d)
 
+    loop(1, NR, lambda d: gather_right(d).start())
     loop(1, NC, lambda d: gather_left(d).start())
-    loop(1, NR, lambda d: gather_right(d).start())
 
     local[0].wait()
     for c in range(C):
@@ -117,6 +119,18 @@
         rt[:, pl.ds(at, BLK)] = rf[pl.ds(at, BLK), :].T[:C].astype(BF)
 
     loop(0, NB, right_turned)
+
+    def make_u(b):
+        at = pl.multiple_of(b * BLK, BLK)
+        slot = lax.rem(b, NU)
+        for q in range(4):
+            u = dot_nn(rb[pl.ds(at, BLK), :C], w1[:, q * 1024 : (q + 1) * 1024]).astype(BF)
+            for j in range(JB):
+                for c in range(8):
+                    row = (q * 8 + c) * S
+                    ub[slot, row : row + S, j * H : (j + 1) * H] = u[j * S : (j + 1) * S, c * H : (c + 1) * H]
+
+    loop(0, NU, make_u)
 
     local[1].wait()
     loop(1, NC, lambda d: gather_left(d).wait())
@@ -134,9 +148,8 @@
             for k in range(2):
                 j = 2 * p + k
                 for c in range(C):
-                    tb[j * S : (j + 1) * S, c * H : (c + 1) * H] = t[c * S : (c + 1) * S, k * H : (k + 1) * H]
-        dwa[...] += dot_nn(rt[:, pl.ds(at, BLK)], tb[...])
-        drf[pl.ds(at, BLK), :] = dot_nn(tb[...], wt[...])
+                    tb[b, j * S : (j + 1) * S, c * H : (c + 1) * H] = t[c * S : (c + 1) * S, k * H : (k + 1) * H]
+        dwa[...] += dot_nn(rt[:, pl.ds(at, BLK)], tb[b])
 
     loop(0, NB, phase1)
 
@@ -149,70 +162,37 @@
     def weight1(d):
         return to_col(dws.at[weight_rows(col_peer(d))], dwr1.at[d - 1], w1_s, w1_r, d)
 
+    def weight2(d):
+        return to_row(dwr2.at[me_r], dwr2.at[me_r], w2_s, w2_r, d)
+
+    def weight3(d):
+        return to_col(dwg.at[weight_rows(me_c)], dwg.at[weight_rows(me_c)], w3_s, w3_r, d)
+
     loop(1, NC, lambda d: weight1(d).start())
-    for s in range(S):
-        drs[s] = drf[pl.ds(s, JL, stride=S), :].T[:C].astype(BF)
-
-    def reduce_right(d):
-        return to_row(drs.at[pl.ds(2 * row_peer(d), 2)], drr.at[d - 1], rsr_s, rsr_r, d)
-
-    loop(1, NR, lambda d: reduce_right(d).start())
-
-    def weight2(d):
-        return to_row(dws2.at[row_peer(d)], dwr2.at[d - 1], w2_s, w2_r, d)
-
-    def weight3(d):
-        return to_row(dwp2, dwp.at[me_r], w3_s, w3_r, d)
-
-    def weight4(d):
-        return to_col(dwg.at[weight_rows(me_c)], dwg.at[weight_rows(me_c)], w4_s, w4_r, d)
 
     def stage_a():
         loop(1, NC, lambda d: weight1(d).wait())
         total = dws[weight_rows(me_c), :].astype(F32)
         for k in range(NC - 1):
             total += dwr1[k].astype(F32)
-        dws2[...] = total.reshape(NR, 8, H)
+        dwr2[me_r] = (total * scale_weight).astype(BF)
         loop(1, NR, lambda d: weight2(d).start())
 
     def stage_b():
         loop(1, NR, lambda d: weight2(d).wait())
-        total = dws2[me_r]
-        for k in range(NR - 1):
-            total += dwr2[k]
-        total = total * scale_weight
-        dwp2[...] = total
-        dwp[me_r] = total
-        loop(1, NR, lambda d: weight3(d).start())
-
-    def stage_c():
-        loop(1, NR, lambda d: weight3(d).wait())
-        dwg[weight_rows(me_c), :] = dwp[...].reshape(64, H).astype(BF)
-        loop(1, NC, lambda d: weight4(d).start())
-
-    def stage_d():
-        loop(1, NR, lambda d: reduce_right(d).wait())
-        total = drs[pl.ds(2 * me_r, 2)].astype(F32)
-        for k in range(NR - 1):
-            total += drr[k].astype(F32)
-        dr_out[...] = total * (1.0 / S)
+        total = dwr2[0].astype(F32)
+        for k in range(1, NR):
+            total += dwr2[k].astype(F32)
+        dwg[weight_rows(me_c), :] = total.astype(BF)
+        loop(1, NC, lambda d: weight3(d).start())
 
     def phase2(b):
-        at = pl.multiple_of(b * BLK, BLK)
-        for q in range(4):
-            u = dot_nn(rb[pl.ds(at, BLK), :C], w1[:, q * 1024 : (q + 1) * 1024]).astype(BF)
-            for j in range(JB):
-                for c in range(8):
-                    row = (q * 8 + c) * S
-                    ub[row : row + S, j * H : (j + 1) * H] = u[j * S : (j + 1) * S, c * H : (c + 1) * H]
+        pl.when(b >= NU)(lambda: make_u(b))
         rhs = jnp.concatenate([gt[b, j] for j in range(JB)], 1)
-        part = dot_nt(ub[...], rhs)
+        part = dot_nt(ub[lax.rem(b, NU)], rhs)
         for k in range(2):
             dla[k] += part[:, k * 128 : (k + 1) * 128]
-        pl.when(b == 2)(stage_a)
-        pl.when(b == 4)(stage_b)
-        pl.when(b == 5)(stage_c)
-        pl.when(b == 6)(stage_d)
+        pl.when(b == STAGE_A)(stage_a)
 
     loop(0, NB, phase2)
 
@@ -224,26 +204,53 @@
         return to_col(dls.at[col_peer(d)], dlr.at[d - 1], rsl_s, rsl_r, d)
 
     loop(1, NC, lambda d: reduce_left(d).start())
-    loop(1, NC, lambda d: weight4(d).wait())
-    dw_out[...] = dwg[...].astype(F32)
+
+    def phase3(b):
+        at = pl.multiple_of(b * BLK, BLK)
+        drf[pl.ds(at, BLK), :] = dot_nn(tb[b], wt[...])
+        pl.when(b == STAGE_B)(stage_b)
+
+    loop(0, NB, phase3)
+
+    for s in range(S):
+        drs[s] = drf[pl.ds(s, JL, stride=S), :].T[:C].astype(BF)
+
+    def reduce_right(d):
+        return to_row(drs.at[pl.ds(2 * row_peer(d), 2)], drr.at[d - 1], rsr_s, rsr_r, d)
+
+    loop(1, NR, lambda d: reduce_right(d).start())
+
     loop(1, NC, lambda d: reduce_left(d).wait())
     total = dls[me_c].astype(F32)
     for k in range(NC - 1):
         total += dlr[k].astype(F32)
     dl_out[0] = total * (1.0 / S)
+    loop(1, NC, lambda d: weight3(d).wait())
+    dw_out[...] = dwg[...]
+    loop(1, NR, lambda d: reduce_right(d).wait())
+    total = drs[pl.ds(2 * me_r, 2)].astype(F32)
+    for k in range(NR - 1):
+        total += drr[k].astype(F32)
+    dr_out[...] = total * (1.0 / S)
+
+
+def hand_out(a, b, c, x, y, z):
+    x[...] = a[...]
+    y[...] = b[...]
+    z[...] = c[...].astype(F32)
 
 
 def on_device(left, right, pair_grad, w_out):
     total_rows = pair_grad.shape[0] * lax.axis_size("row")
     total_cols = pair_grad.shape[1] * lax.axis_size("col")
     scale_weight = 1.0 / (float(total_rows) * float(total_cols)) ** 0.5
-    sems = [pltpu.SemaphoreType.DMA((n - 1,)) for n in (NC, NR, NR, NC, NR, NR, NC, NC) for _ in range(2)]
-    return pl.pallas_call(
+    sems = [pltpu.SemaphoreType.DMA((n - 1,)) for n in (NC, NR, NR, NC, NR, NC, NC) for _ in range(2)]
+    grads = pl.pallas_call(
         functools.partial(kernel, scale_weight),
         out_shape=(
             jax.ShapeDtypeStruct((1, C, IL), F32),
             jax.ShapeDtypeStruct((2, C, JL), F32),
-            jax.ShapeDtypeStruct((C * C, H), F32),
+            jax.ShapeDtypeStruct((C * C, H), BF),
         ),
         in_specs=[pl.BlockSpec(memory_space=pl.ANY)] * 4,
         out_specs=[pl.BlockSpec(memory_space=pltpu.VMEM)] * 3,
@@ -260,18 +267,15 @@
             pltpu.VMEM((C, JL * S), BF),
             pltpu.VMEM((C, C * H), BF),
             pltpu.VMEM((C * H, 128), BF),
-            pltpu.VMEM((BLK, C * H), BF),
-            pltpu.VMEM((C * S, JB * H), BF),
+            pltpu.VMEM((NB, BLK, C * H), BF),
+            pltpu.VMEM((NU, C * S, JB * H), BF),
             pltpu.VMEM((JL * S, 128), F32),
             pltpu.VMEM((S, C, JL), BF),
             pltpu.VMEM((NR - 1, 2, C, JL), BF),
             pltpu.VMEM((C, C * H), F32),
             pltpu.VMEM((C * C, H), BF),
             pltpu.VMEM((NC - 1, 64, H), BF),
-            pltpu.VMEM((NR, 8, H), F32),
-            pltpu.VMEM((NR, 8, H), F32),
-            pltpu.VMEM((NR - 1, 8, H), F32),
-            pltpu.VMEM((8, H), F32),
+            pltpu.VMEM((NR, 64, H), BF),
             pltpu.VMEM((C * C, H), BF),
             pltpu.VMEM((2, C * S, 128), F32),
             pltpu.VMEM((S, C, IL), BF),
@@ -285,6 +289,11 @@
         ),
         name="outer_product_mean_grad",
     )(left, right, pair_grad, w_out)
+    return pl.pallas_call(
+        hand_out,
+        out_shape=tuple(jax.ShapeDtypeStruct(g.shape, F32) for g in grads),
+        name="hand_out",
+    )(*grads)
 
 
 def solution(mesh):

time: 61.2 us -> 52.5 us (0.86)
  the two profiles are of different devices: /device:TPU:1 before, /device:TPU:0 now
where the time goes in v2:
time: 52.5 us; the launch traced here: 52.4 us
  Pallas kernels  51.8 us (99%)
  between operations  0.64 us (1%)
    pallas_call x1, Pallas kernels, on_device(): pl.pallas_call(functools.partial(kernel, scale_weight), out_shape=(jax.Sh...  49.9 us
    pallas_call x1, Pallas kernels, on_device(): pl.pallas_call(hand_out, out_shape=tuple((jax.ShapeDtypeStruct(g.shape, F...  1.82 us

profile of v2, /device:TPU:0, one launch (start us, length us, event | category | flops | bytes accessed | tf_op | source)
XLA Modules:
  0.0 52.4 jit_solution(16467220394107512240)
XLA Ops:
  0.6 49.9 %outer_product_mean_grad.1 = (f32[1,32,256]{2,1,0:T(8,128)}, f32[2,32,128]{2,1,0:T(8,128)}, bf16[1024,128]{1,0:T(8,128)(2,1)}) custom-call(bf16[1,32,256]{2,1,0:T(8,128)(2,1)} %left_hbm.1, bf16[2,32,128]{2,1,0:T(8,128)(2,1)} %right_hbm.1, bf16[256,128,128]{2,1,0:T(8,128)(2,1)} %g_hbm.1, bf16[1024,128]{1,0:T(8,128)(2,1)} %w_hbm.1), custom_call_target="tpu_custom_call" | custom-call | tf_op jit(solution)/shard_map/outer_product_mean_grad/pallas_call | solution.py:248
  50.6 1.8 %hand_out.1 = (f32[1,32,256]{2,1,0:T(8,128)}, f32[2,32,128]{2,1,0:T(8,128)}, f32[1024,128]{1,0:T(8,128)}) custom-call(f32[1,32,256]{2,1,0:T(8,128)} %get-tuple-element.6.a, f32[2,32,128]{2,1,0:T(8,128)} %get-tuple-element.7.b, bf16[1024,128]{1,0:T(8,128)(2,1)} %get-tuple-element.8.c), custom_call_target="tpu_custom_call" | custom-call | tf_op jit(solution)/shard_map/hand_out/pallas_call | solution.py:292

commit v3 on v2

--- a/solution.py
+++ b/solution.py
@@ -15,16 +15,15 @@
 JB = 16
 NB = JL // JB
 BLK = JB * S
-NU = 3
-STAGE_A, STAGE_B = 5, 3
-
-
-def dot_nn(a, b):
-    return jnp.dot(a, b, preferred_element_type=F32)
-
-
-def dot_nt(a, b):
-    return lax.dot_general(a, b, (((1,), (1,)), ((), ())), preferred_element_type=F32)
+NU = 5
+STAGE_A, STAGE_B = 6, 11
+
+
+push, acc_lhs, pop = pltpu.matmul_push_rhs, pltpu.matmul_acc_lhs, pltpu.matmul_pop
+
+
+def acc(rows, count):
+    return [pltpu.ACC(m)((rows, 256), F32) for m in range(2) for _ in range(count)]
 
 
 def loop(lower, upper, body):
@@ -40,7 +39,7 @@
     left_hbm, right_hbm, g_hbm, w_hbm,
     dl_out, dr_out, dw_out,
     w_v, lg, rg, g_in, gt, lf, lb, rf, rb, rt, w1, wt, tb, ub,
-    drf, drs, drr, dwa, dws, dwr1, dwr2, dwg, dla, dls, dlr,
+    drf, drs, drr, dws, dwr1, dwr2, dwg, dla, dls, dlr,
     g_sem, in_sem,
     agl_s, agl_r, agr_s, agr_r, rsr_s, rsr_r, w1_s, w1_r, w2_s, w2_r, w3_s, w3_r, rsl_s, rsl_r,
 ):
@@ -92,13 +91,14 @@
     loop(1, NR, lambda d: gather_right(d).start())
     loop(1, NC, lambda d: gather_left(d).start())
 
+    w1[...] = jnp.zeros_like(w1)
+    wt[...] = jnp.zeros_like(wt)
+    rb[:, 128:] = jnp.zeros_like(rb[:, 128:])
     local[0].wait()
     for c in range(C):
-        w1[:, c * H : (c + 1) * H] = w_v[c * C : (c + 1) * C, :]
+        w1[:C, c * H : (c + 1) * H] = w_v[c * C : (c + 1) * C, :]
         block = w_v[c * C : (c + 1) * C, :].astype(F32)
-        wt[c * H : (c + 1) * H, :] = jnp.concatenate([block, jnp.zeros((128 - C, H), F32)], 0).T.astype(BF)
-    dwa[...] = jnp.zeros_like(dwa)
-    dla[...] = jnp.zeros_like(dla)
+        wt[c * H : (c + 1) * H, :128] = jnp.concatenate([block, jnp.zeros((128 - C, H), F32)], 0).T.astype(BF)
 
     def turn(b):
         g_copy(b).wait()
@@ -112,7 +112,7 @@
     for s in range(S):
         block = jnp.concatenate([rg[s].astype(F32), jnp.zeros((128 - C, JL), F32)], 0)
         rf[pl.ds(s, JL, stride=S), :] = block.T
-    rb[...] = rf[...].astype(BF)
+    rb[:, :128] = rf[...].astype(BF)
 
     def right_turned(b):
         at = pl.multiple_of(b * BLK, BLK)
@@ -120,17 +120,32 @@
 
     loop(0, NB, right_turned)
 
-    def make_u(b):
+    def make_u(b, regions):
         at = pl.multiple_of(b * BLK, BLK)
         slot = lax.rem(b, NU)
-        for q in range(4):
-            u = dot_nn(rb[pl.ds(at, BLK), :C], w1[:, q * 1024 : (q + 1) * 1024]).astype(BF)
-            for j in range(JB):
-                for c in range(8):
-                    row = (q * 8 + c) * S
+        pending = []
+
+        def take():
+            q = pending.pop(0)
+            u = pop(regions[q % 2][q // 2 % 2]).astype(BF)
+            for c in range(2):
+                for j in range(JB):
+                    row = (2 * q + c) * S
                     ub[slot, row : row + S, j * H : (j + 1) * H] = u[j * S : (j + 1) * S, c * H : (c + 1) * H]
 
-    loop(0, NU, make_u)
+        for q in range(C // 2):
+            push(w1[:, q * 256 : (q + 1) * 256], q // 2 % 2, q % 2)
+            if len(pending) >= 2:
+                take()
+            acc_lhs(regions[q % 2][q // 2 % 2], rb[pl.ds(at, BLK), :], q // 2 % 2)
+            pending.append(q)
+        while pending:
+            take()
+
+    def early(*accs):
+        loop(0, NU, lambda b: make_u(b, (accs[0:2], accs[2:4])))
+
+    pl.run_scoped(early, *acc(256, 2))
 
     local[1].wait()
     loop(1, NC, lambda d: gather_left(d).wait())
@@ -140,21 +155,48 @@
     for k in range(2):
         lb[:, k * 128 : (k + 1) * 128] = lf[k].astype(BF)
 
-    def phase1(b):
-        at = pl.multiple_of(b * BLK, BLK)
-        for p in range(JB // 2):
-            rhs = jnp.concatenate([gt[b, 2 * p], gt[b, 2 * p + 1]], 1)
-            t = dot_nn(lb[...], rhs).astype(BF)
+    def pair(b, p):
+        return jnp.concatenate([gt[b, 2 * p], gt[b, 2 * p + 1]], 1)
+
+    def phase1(*accs):
+        t_acc, w_acc = (accs[0:3], accs[3:6]), (accs[6:14], accs[14:22])
+
+        def block(b):
+            at = pl.multiple_of(b * BLK, BLK)
+            pending, used = [], [0, 0]
+
+            def take():
+                region, p, half = pending.pop(0)
+                t = pop(region).astype(BF)
+                for k in range(2):
+                    j = 2 * p + k
+                    for c in range(C // 2):
+                        cc = half * (C // 2) + c
+                        tb[b, j * S : (j + 1) * S, cc * H : (cc + 1) * H] = t[c * S : (c + 1) * S, k * H : (k + 1) * H]
+
+            for p in range(JB // 2):
+                m = p % 2
+                push(pair(b, p), p // 2 % 2, m)
+                for half in range(2):
+                    region = t_acc[m][used[m] % 3]
+                    used[m] += 1
+                    if len(pending) >= 4:
+                        take()
+                    acc_lhs(region, lb[half * 256 : (half + 1) * 256, :], p // 2 % 2 if half == 0 else None)
+                    pending.append((region, p, half))
+            while pending:
+                take()
+            for q in range(C // 2):
+                push(tb[b, :, q * 256 : (q + 1) * 256], q // 2 % 2, q % 2)
+                acc_lhs(w_acc[q % 2][q // 2], rt[:, pl.ds(at, BLK)], q // 2 % 2)
+
+        loop(0, NB, block)
+        for q in range(C // 2):
+            part = pop(w_acc[q % 2][q // 2]).astype(BF)
             for k in range(2):
-                j = 2 * p + k
-                for c in range(C):
-                    tb[b, j * S : (j + 1) * S, c * H : (c + 1) * H] = t[c * S : (c + 1) * S, k * H : (k + 1) * H]
-        dwa[...] += dot_nn(rt[:, pl.ds(at, BLK)], tb[b])
-
-    loop(0, NB, phase1)
-
-    for c in range(C):
-        dws[c * C : (c + 1) * C, :] = dwa[:, c * H : (c + 1) * H].astype(BF)
+                dws[(2 * q + k) * C : (2 * q + k + 1) * C, :] = part[:, k * H : (k + 1) * H]
+
+    pl.run_scoped(phase1, *acc(256, 3), *acc(C, 8))
 
     def weight_rows(k):
         return pl.ds(pl.multiple_of(k * 64, 64), 64)
@@ -186,16 +228,23 @@
         dwg[weight_rows(me_c), :] = total.astype(BF)
         loop(1, NC, lambda d: weight3(d).start())
 
-    def phase2(b):
-        pl.when(b >= NU)(lambda: make_u(b))
-        rhs = jnp.concatenate([gt[b, j] for j in range(JB)], 1)
-        part = dot_nt(ub[lax.rem(b, NU)], rhs)
+    def phase2(*accs):
+        l_acc, u_acc = accs[0:2], (accs[2:4], accs[4:6])
+
+        def block(b):
+            pl.when(b >= NU)(lambda: make_u(b, u_acc))
+            slot = lax.rem(b, NU)
+            for p in range(JB // 2):
+                push(pair(b, p), p // 2 % 2, p % 2, transpose=True)
+                acc_lhs(l_acc[p % 2], ub[slot, :, p * 256 : (p + 1) * 256], p // 2 % 2)
+            pl.when(b == STAGE_A)(stage_a)
+
+        loop(0, NB, block)
+        part = pop(l_acc[0]) + pop(l_acc[1])
         for k in range(2):
-            dla[k] += part[:, k * 128 : (k + 1) * 128]
-        pl.when(b == STAGE_A)(stage_a)
-
-    loop(0, NB, phase2)
-
+            dla[k] = part[:, k * 128 : (k + 1) * 128]
+
+    pl.run_scoped(phase2, *acc(C * S, 1), *acc(256, 2))
     for s in range(S):
         for k in range(2):
             dls[s, :, k * 128 : (k + 1) * 128] = dla[k, pl.ds(s, C, stride=S), :].astype(BF)
@@ -205,20 +254,36 @@
 
     loop(1, NC, lambda d: reduce_left(d).start())
 
-    def phase3(b):
-        at = pl.multiple_of(b * BLK, BLK)
-        drf[pl.ds(at, BLK), :] = dot_nn(tb[b], wt[...])
-        pl.when(b == STAGE_B)(stage_b)
-
-    loop(0, NB, phase3)
-
-    for s in range(S):
-        drs[s] = drf[pl.ds(s, JL, stride=S), :].T[:C].astype(BF)
+    def phase3(*accs):
+        r_acc = accs[0:4], accs[4:8]
+        for q in range(C // 2):
+            for m in range(2):
+                push(wt[q * 256 : (q + 1) * 256, :], q % 2, m)
+                for k in range(4):
+                    acc_lhs(r_acc[m][k], tb[4 * m + k, :, q * 256 : (q + 1) * 256], q % 2 if k == 0 else None)
+            if q == STAGE_B:
+                stage_b()
+        for m in range(2):
+            for k in range(4):
+                at = (4 * m + k) * BLK
+                drf[at : at + BLK, :] = pop(r_acc[m][k])[:, :128]
+
+    pl.run_scoped(phase3, *acc(256, 4))
 
     def reduce_right(d):
         return to_row(drs.at[pl.ds(2 * row_peer(d), 2)], drr.at[d - 1], rsr_s, rsr_r, d)
 
-    loop(1, NR, lambda d: reduce_right(d).start())
+    def right_piece(d):
+        for k in range(2):
+            s = 2 * row_peer(d) + k
+            drs[s] = drf[pl.ds(s, JL, stride=S), :].T[:C].astype(BF)
+
+    def right_out(d):
+        right_piece(d)
+        reduce_right(d).start()
+
+    loop(1, NR, right_out)
+    right_piece(0)
 
     loop(1, NC, lambda d: reduce_left(d).wait())
     total = dls[me_c].astype(F32)
@@ -248,9 +313,9 @@
     grads = pl.pallas_call(
         functools.partial(kernel, scale_weight),
         out_shape=(
-            jax.ShapeDtypeStruct((1, C, IL), F32),
-            jax.ShapeDtypeStruct((2, C, JL), F32),
-            jax.ShapeDtypeStruct((C * C, H), BF),
+            pltpu.VMEM((1, C, IL), F32),
+            pltpu.VMEM((2, C, JL), F32),
+            pltpu.VMEM((C * C, H), BF),
         ),
         in_specs=[pl.BlockSpec(memory_space=pl.ANY)] * 4,
         out_specs=[pl.BlockSpec(memory_space=pltpu.VMEM)] * 3,
@@ -263,16 +328,15 @@
             pltpu.VMEM((2, C * S, 128), F32),
             pltpu.VMEM((C * S, IL), BF),
             pltpu.VMEM((JL * S, 128), F32),
-            pltpu.VMEM((JL * S, 128), BF),
+            pltpu.VMEM((JL * S, 256), BF),
             pltpu.VMEM((C, JL * S), BF),
-            pltpu.VMEM((C, C * H), BF),
-            pltpu.VMEM((C * H, 128), BF),
+            pltpu.VMEM((256, C * H), BF),
+            pltpu.VMEM((C * H, 256), BF),
             pltpu.VMEM((NB, BLK, C * H), BF),
             pltpu.VMEM((NU, C * S, JB * H), BF),
             pltpu.VMEM((JL * S, 128), F32),
             pltpu.VMEM((S, C, JL), BF),
             pltpu.VMEM((NR - 1, 2, C, JL), BF),
-            pltpu.VMEM((C, C * H), F32),
             pltpu.VMEM((C * C, H), BF),
             pltpu.VMEM((NC - 1, 64, H), BF),
             pltpu.VMEM((NR, 64, H), BF),
@@ -292,8 +356,10 @@
     return pl.pallas_call(
         hand_out,
         out_shape=tuple(jax.ShapeDtypeStruct(g.shape, F32) for g in grads),
+        in_specs=[pl.BlockSpec(memory_space=pltpu.VMEM)] * 3,
+        out_specs=[pl.BlockSpec(memory_space=pltpu.VMEM)] * 3,
         name="hand_out",
-    )(*grads)
+    )(*[pltpu.with_memory_space_constraint(g, pltpu.VMEM) for g in grads])
 
 
 def solution(mesh):

time: 52.5 us -> 48.3 us (0.920)
  Pallas kernels: 51.8 us -> 47.6 us
    pallas_call x1, Pallas kernels: 49.9 us -> 46.8 us  [on_device(): pl.pallas_call(functools.partial(kernel, scale_weight), out_shape=(pltpu....]
    pallas_call x1, Pallas kernels: 1.82 us -> 0.84 us  [on_device(): pl.pallas_call(hand_out, out_shape=tuple((jax.ShapeDtypeStruct(g.shape, F...]
where the time goes in v3:
time: 48.3 us; the launch traced here: 48.2 us
  Pallas kernels  47.6 us (99%)
  between operations  0.64 us (1%)
    pallas_call x1, Pallas kernels, on_device(): pl.pallas_call(functools.partial(kernel, scale_weight), out_shape=(pltpu....  46.8 us

profile of v3, /device:TPU:0, one launch (start us, length us, event | category | flops | bytes accessed | tf_op | source)
XLA Modules:
  0.0 48.2 jit_solution(13903069134889524543)
XLA Ops:
  0.6 46.8 %outer_product_mean_grad.1 = (f32[1,32,256]{2,1,0:T(8,128)S(1)}, f32[2,32,128]{2,1,0:T(8,128)S(1)}, bf16[1024,128]{1,0:T(8,128)(2,1)S(1)}) custom-call(bf16[1,32,256]{2,1,0:T(8,128)(2,1)} %left_hbm.1, bf16[2,32,128]{2,1,0:T(8,128)(2,1)} %right_hbm.1, bf16[256,128,128]{2,1,0:T(8,128)(2,1)} %g_hbm.1, bf16[1024,128]{1,0:T(8,128)(2,1)} %w_hbm.1), custom_call_target="tpu_custom_call" | custom-call | tf_op jit(solution)/shard_map/outer_product_mean_grad/pallas_call | solution.py:313
  47.4 0.8 %hand_out.1 = (f32[1,32,256]{2,1,0:T(8,128)}, f32[2,32,128]{2,1,0:T(8,128)}, f32[1024,128]{1,0:T(8,128)}) custom-call(f32[1,32,256]{2,1,0:T(8,128)S(1)} %get-tuple-element.6.a, f32[2,32,128]{2,1,0:T(8,128)S(1)} %get-tuple-element.7.b, bf16[1024,128]{1,0:T(8,128)(2,1)S(1)} %get-tuple-element.8.c), custom_call_target="tpu_custom_call" | custom-call | tf_op jit(solution)/shard_map/hand_out/pallas_call | solution.py:356

commit v4 on v3

--- a/solution.py
+++ b/solution.py
@@ -17,6 +17,7 @@
 BLK = JB * S
 NU = 5
 STAGE_A, STAGE_B = 6, 11
+ROWS, COLS = tuple(range(1, NR)), tuple(range(1, NC))
 
 
 push, acc_lhs, pop = pltpu.matmul_push_rhs, pltpu.matmul_acc_lhs, pltpu.matmul_pop
@@ -24,6 +25,11 @@
 
 def acc(rows, count):
     return [pltpu.ACC(m)((rows, 256), F32) for m in range(2) for _ in range(count)]
+
+
+def each(order, body):
+    for k in order:
+        body(k)
 
 
 def loop(lower, upper, body):
@@ -65,8 +71,8 @@
         )
 
     barrier = pltpu.get_barrier_semaphore()
-    loop(1, NR, lambda d: pl.semaphore_signal(barrier, inc=1, device_id=(row_peer(d), me_c), device_id_type=MESH))
-    loop(1, NC, lambda d: pl.semaphore_signal(barrier, inc=1, device_id=(me_r, col_peer(d)), device_id_type=MESH))
+    each(ROWS, lambda d: pl.semaphore_signal(barrier, inc=1, device_id=(row_peer(d), me_c), device_id_type=MESH))
+    each(COLS, lambda d: pl.semaphore_signal(barrier, inc=1, device_id=(me_r, col_peer(d)), device_id_type=MESH))
 
     def g_copy(b):
         at = pl.multiple_of(b * JB, JB)
@@ -88,8 +94,8 @@
     def gather_right(d):
         return to_row(right_hbm, rg.at[pl.ds(2 * me_r, 2)], agr_s, agr_r, d)
 
-    loop(1, NR, lambda d: gather_right(d).start())
-    loop(1, NC, lambda d: gather_left(d).start())
+    each(ROWS, lambda d: gather_right(d).start())
+    each(COLS, lambda d: gather_left(d).start())
 
     w1[...] = jnp.zeros_like(w1)
     wt[...] = jnp.zeros_like(wt)
@@ -108,7 +114,7 @@
     loop(0, NB, turn)
 
     local[2].wait()
-    loop(1, NR, lambda d: gather_right(d).wait())
+    each(ROWS, lambda d: gather_right(d).wait())
     for s in range(S):
         block = jnp.concatenate([rg[s].astype(F32), jnp.zeros((128 - C, JL), F32)], 0)
         rf[pl.ds(s, JL, stride=S), :] = block.T
@@ -148,10 +154,17 @@
     pl.run_scoped(early, *acc(256, 2))
 
     local[1].wait()
-    loop(1, NC, lambda d: gather_left(d).wait())
-    for s in range(S):
+
+    def left_rows(s):
         for k in range(2):
             lf[k, pl.ds(s, C, stride=S), :] = lg[s, :, k * 128 : (k + 1) * 128].astype(F32)
+
+    def left_arrived(d):
+        gather_left(d).wait()
+        left_rows(lax.rem(me_c + NC - d, NC))
+
+    left_rows(me_c)
+    each(COLS, left_arrived)
     for k in range(2):
         lb[:, k * 128 : (k + 1) * 128] = lf[k].astype(BF)
 
@@ -210,23 +223,23 @@
     def weight3(d):
         return to_col(dwg.at[weight_rows(me_c)], dwg.at[weight_rows(me_c)], w3_s, w3_r, d)
 
-    loop(1, NC, lambda d: weight1(d).start())
+    each(COLS, lambda d: weight1(d).start())
 
     def stage_a():
-        loop(1, NC, lambda d: weight1(d).wait())
+        each(COLS, lambda d: weight1(d).wait())
         total = dws[weight_rows(me_c), :].astype(F32)
         for k in range(NC - 1):
             total += dwr1[k].astype(F32)
         dwr2[me_r] = (total * scale_weight).astype(BF)
-        loop(1, NR, lambda d: weight2(d).start())
+        each(ROWS, lambda d: weight2(d).start())
 
     def stage_b():
-        loop(1, NR, lambda d: weight2(d).wait())
+        each(ROWS, lambda d: weight2(d).wait())
         total = dwr2[0].astype(F32)
         for k in range(1, NR):
             total += dwr2[k].astype(F32)
         dwg[weight_rows(me_c), :] = total.astype(BF)
-        loop(1, NC, lambda d: weight3(d).start())
+        each(COLS, lambda d: weight3(d).start())
 
     def phase2(*accs):
         l_acc, u_acc = accs[0:2], (accs[2:4], accs[4:6])
@@ -252,7 +265,7 @@
     def reduce_left(d):
         return to_col(dls.at[col_peer(d)], dlr.at[d - 1], rsl_s, rsl_r, d)
 
-    loop(1, NC, lambda d: reduce_left(d).start())
+    each(COLS, lambda d: reduce_left(d).start())
 
     def phase3(*accs):
         r_acc = accs[0:4], accs[4:8]
@@ -282,17 +295,17 @@
         right_piece(d)
         reduce_right(d).start()
 
-    loop(1, NR, right_out)
+    each(ROWS, right_out)
     right_piece(0)
 
-    loop(1, NC, lambda d: reduce_left(d).wait())
+    each(COLS, lambda d: reduce_left(d).wait())
     total = dls[me_c].astype(F32)
     for k in range(NC - 1):
         total += dlr[k].astype(F32)
     dl_out[0] = total * (1.0 / S)
-    loop(1, NC, lambda d: weight3(d).wait())
+    each(COLS, lambda d: weight3(d).wait())
     dw_out[...] = dwg[...]
-    loop(1, NR, lambda d: reduce_right(d).wait())
+    each(ROWS, lambda d: reduce_right(d).wait())
     total = drs[pl.ds(2 * me_r, 2)].astype(F32)
     for k in range(NR - 1):
         total += drr[k].astype(F32)

time: 48.3 us -> 48.2 us (level)
  no operation moved by 1% of the time
where the time goes in v4:
time: 48.2 us; the launch traced here: 48.1 us
  Pallas kernels  47.4 us (98%)
  between operations  0.64 us (1%)
    pallas_call x1, Pallas kernels, on_device(): pl.pallas_call(functools.partial(kernel, scale_weight), out_shape=(pltpu....  46.6 us

profile of v4, /device:TPU:0, one launch (start us, length us, event | category | flops | bytes accessed | tf_op | source)
XLA Modules:
  0.0 48.1 jit_solution(2628255913920087703)
XLA Ops:
  0.6 46.6 %outer_product_mean_grad.1 = (f32[1,32,256]{2,1,0:T(8,128)S(1)}, f32[2,32,128]{2,1,0:T(8,128)S(1)}, bf16[1024,128]{1,0:T(8,128)(2,1)S(1)}) custom-call(bf16[1,32,256]{2,1,0:T(8,128)(2,1)} %left_hbm.1, bf16[2,32,128]{2,1,0:T(8,128)(2,1)} %right_hbm.1, bf16[256,128,128]{2,1,0:T(8,128)(2,1)} %g_hbm.1, bf16[1024,128]{1,0:T(8,128)(2,1)} %w_hbm.1), custom_call_target="tpu_custom_call" | custom-call | tf_op jit(solution)/shard_map/outer_product_mean_grad/pallas_call | solution.py:326
  47.2 0.8 %hand_out.1 = (f32[1,32,256]{2,1,0:T(8,128)}, f32[2,32,128]{2,1,0:T(8,128)}, f32[1024,128]{1,0:T(8,128)}) custom-call(f32[1,32,256]{2,1,0:T(8,128)S(1)} %get-tuple-element.6.a, f32[2,32,128]{2,1,0:T(8,128)S(1)} %get-tuple-element.7.b, bf16[1024,128]{1,0:T(8,128)(2,1)S(1)} %get-tuple-element.8.c), custom_call_target="tpu_custom_call" | custom-call | tf_op jit(solution)/shard_map/hand_out/pallas_call | solution.py:369
